TPU v7x, 32 devices: a whole 2x2x4 slice. The times are simulated.
32 devices in a mesh: grp: 2 (over y), step: 4 (over z), chain: 2 (over x), rep: 2 (over core).
Axes of the slice: x: 2, y: 2, z: 4, core: 2. Of those that a mesh axis runs over, the one named last changes fastest.
Arguments:
- init_seed: int32 [8], P(('grp', 'chain', 'rep')), parts along dimension 0, may hold values from 0 to 63
- noise_index: int32 [8, 32], P(('grp', 'chain', 'rep'), 'step'), parts along dimension 0, may hold values from 0 to 4095
- init_table: float32 [64, 256], replicated, may hold values from -6 to 6
- noise_table: float32 [4096, 256], replicated, may hold values from -6 to 6
- weight: float32 [256, 256], replicated
- bias: float32 [256], replicated, may hold values from -3 to 3
- rates: float32 [64, 256], P(('grp', 'step')), parts along dimension 0, may hold values from 0 to 0.5
- old_path: float32 [8, 32, 256], P(('grp', 'chain', 'rep'), 'step'), parts along dimension 0, may hold values from -6 to 6
- cotangent: float32 [8, 32, 256], P(('grp', 'chain', 'rep'), 'step'), parts along dimension 0, may hold values from -0.3 to 0.3
Outputs:
- path_new: float32 [8, 32, 256], P(('grp', 'chain', 'rep'), 'step'), parts along dimension 0
- grad_w: float32 [512, 256], P('grp'), parts along dimension 0
- grad_b: float32 [512], P('grp'), parts along dimension 0
There are 2 independent parts, one for each index of `grp`. A program takes and returns all parts, laid end to end along the dimension named above; an argument that names none is the same for every part. Nothing has to cross between parts.
All inputs are finite; a program needn't handle non-finite values.
Results may differ from a plain program's by a relative error of at most 0.0001.
Values sent between devices are 32-bit elements; how exact they have to be, the bound alone decides.
A program may use at most 64 MiB of HBM per device.

v0:
```python
import jax
import jax.numpy as jnp
from jax import lax
from jax.sharding import PartitionSpec as P


def shifted_2(block, axis, distance):
    devices = range(lax.axis_size(axis))
    route = [(i - distance, i) for i in devices if i - distance in devices]
    return lax.ppermute(block, axis, route)


def carried_in(x, axis, combine, identity, reverse):
    length, mine = (lax.axis_size(axis), lax.axis_index(axis))
    everything = jax.tree.map(lambda part: lax.all_gather(part, axis), x)
    start = jax.tree.map(
        lambda part, zero: jnp.broadcast_to(jnp.asarray(zero, part.dtype), part.shape), x, identity
    )

    def turn(k, before):
        at = length - 1 - k if reverse else k
        reached = at > mine if reverse else at < mine
        new = combine(before, jax.tree.map(lambda part: part[at], everything))
        return jax.tree.map(lambda a, b: jnp.where(reached, a, b), new, before)

    return lax.fori_loop(0, length, turn, start)


def compose(earlier, later):
    early_mat, early_vec = earlier
    late_mat, late_vec = later
    highest = lax.Precision.HIGHEST
    new_mat = jnp.einsum("...ij,...jk->...ik", late_mat, early_mat, precision=highest)
    new_vec = jnp.einsum("...ij,...j->...i", late_mat, early_vec, precision=highest) + late_vec
    return (new_mat, new_vec)


def shards(
    init_seed, noise_index, init_table, noise_table, weight, bias, rates, old_path, cotangent
):
    highest = lax.Precision.HIGHEST
    chains, steps, width = old_path.shape
    ranks = lax.axis_size("step")
    position = lax.axis_index("step")
    step_size = 4.0 / (steps * ranks)
    start_state = init_table[init_seed]
    shifted = shifted_2(old_path[:, -1], "step", 1)
    first_prev = jnp.where(position == 0, start_state, shifted)
    previous = jnp.concatenate([first_prev[:, None], old_path[:, :-1]], axis=1)
    mixed = jnp.einsum("ctj,ij->cti", previous, weight, precision=highest)
    squash = jnp.tanh(mixed + bias + noise_table[noise_index])
    slope = 1.0 - squash * squash
    keep_rate = 1.0 - rates
    offset = step_size * (squash - slope * mixed)
    identity = jnp.eye(width, dtype=jnp.float32)
    jacobian = keep_rate[None, :, :, None] * identity + step_size * slope[:, :, :, None] * weight
    prefix_mat, prefix_vec = lax.associative_scan(compose, (jacobian, offset), axis=1)
    transposed = jnp.swapaxes(jacobian, 2, 3)
    source = jnp.einsum("ctij,ctj->cti", transposed, cotangent, precision=highest)
    flip_mat, flip_vec = lax.associative_scan(
        compose, (jnp.flip(transposed, 1), jnp.flip(source, 1)), axis=1
    )
    suffix_mat = jnp.flip(flip_mat, 1)
    suffix_vec = jnp.flip(flip_vec, 1)
    block_mat = prefix_mat[:, -1]
    block_vec = prefix_vec[:, -1]
    back_vec = suffix_vec[:, 0]
    neutral = (jnp.broadcast_to(identity, block_mat.shape), jnp.zeros_like(block_vec))
    ahead_mat, ahead_vec = carried_in((block_mat, block_vec), "step", compose, neutral, False)
    entry_state = jnp.einsum("cij,cj->ci", ahead_mat, start_state, precision=highest) + ahead_vec
    behind_mat, adjoint_in = carried_in(
        (suffix_mat[:, 0], back_vec), "step", compose, neutral, True
    )
    path_new = jnp.einsum("ctij,cj->cti", prefix_mat, entry_state, precision=highest) + prefix_vec
    carried = jnp.einsum("ctij,cj->cti", suffix_mat, adjoint_in, precision=highest) + suffix_vec
    following = jnp.concatenate([carried[:, 1:], adjoint_in[:, None]], axis=1)
    adjoint = cotangent + following
    weighted = adjoint * slope
    grad_local = step_size * jnp.einsum("cti,ctj->ij", weighted, previous, precision=highest)
    bias_local = step_size * jnp.sum(weighted, axis=(0, 1))
    grad_w, grad_b = lax.psum((grad_local, bias_local), ("step", "chain", "rep"))
    return (path_new, grad_w, grad_b)


def solution(mesh):
    placed = (
        P(("grp", "chain", "rep")),
        P(("grp", "chain", "rep"), "step"),
        P(),
        P(),
        P(),
        P(),
        P(("grp", "step"), None),
        P(("grp", "chain", "rep"), "step", None),
        P(("grp", "chain", "rep"), "step", None),
    )
    return jax.shard_map(
        shards,
        mesh=mesh,
        in_specs=placed,
        out_specs=(P(("grp", "chain", "rep"), "step", None), P("grp", None), P("grp")),
        check_vma=False,
    )
```

profile of v0, /device:TPU:1, one launch (start us, length us, event | category | flops | bytes accessed | tf_op | source)
XLA Modules:
  0.0 272.3 jit_solution(16754340663512875002)
XLA Ops:
  8.0 4.0 %collective-permute-start = (f32[1,256]{1,0:T(1,128)S(1)}, f32[1,256]{1,0:T(1,128)S(1)}, u32[]{:S(2)}, u32[]{:S(2)}) collective-permute-start(f32[1,256]{1,0:T(1,128)S(1)} %slice_bitcast_fusion.12), channel_id=1, source_target_pairs={{0,4},{4,8},{8,12},{1,5},{5,9},{9,13},{2,6},{6,10},{10,14},{3,7},{... | collective-permute-start | bytes 3080 | tf_op jit(solution)/shard_map/ppermute | solution.py:10
  13.4 2.8 %gather_fusion = f32[8,256]{1,0:T(8,128)S(1)} fusion(f32[4096,256]{1,0:T(8,128)} %param.16, s32[1024]{0:T(1024)S(1)} %pad_clamp_fusion), kind=kCustom, calls=%fused_computation | custom fusion | bytes 16416 | tf_op jit(solution)/shard_map/gather | solution.py:51
  18.9 2.4 fusion.21
  37.3 2.8 %pad.79 = f32[1,4,256,256]{3,2,1,0:T(8,128)} pad(f32[1,2,256,256]{3,2,1,0:T(8,128)} %pad_add_fusion.1, f32[]{:T(128)} %constant.88.clone.1), padding=0_0_0x1_0_1x0_0_0x0_0_0 | pad | bytes 1572868 | tf_op jit(solution)/shard_map/pad | solution.py:57
  40.1 3.1 %convolution_bitcast_fusion.4 = f32[1,3,256,256]{3,2,1,0:T(8,128)} fusion(f32[1,4,256,256]{3,2,1,0:T(8,128)} %pad.79, f32[1,4,256,256]{3,2,1,0:T(8,128)S(1)} %pad.78, f32[1,8,256,256]{3,2,1,0:T(8,128)S(1)} %get-tuple-element.325), kind=kOutput, calls=%fused_computation.38 | convolution fusion | flops 604176384 | bytes 3145728 | tf_op jit(solution)/shard_map/...ij,...jk->...ik/dot_general | solution.py:33
  44.3 2.3 slice.227
  46.6 3.4 %convolution_bitcast_fusion.1 = f32[1,4,256,256]{3,2,1,0:T(8,128)S(1)} fusion(f32[1,4,256,256]{2,3,1,0:T(8,128)} %slice.227, f32[1,4,256,256]{2,3,1,0:T(8,128)} %copy-done.3), kind=kOutput, calls=%fused_computation.35 | convolution fusion | flops 805306368 | bytes 3145728 | tf_op jit(solution)/shard_map/...ij,...jk->...ik/dot_general | solution.py:33
  52.2 2.1 slice.223
  55.1 2.3 pad_maximum_fusion
  57.4 2.2 pad.80
  59.6 4.7 %pad.81 = f32[1,8,256,256]{3,2,1,0:T(8,128)} pad(f32[1,4,256,256]{3,2,1,0:T(8,128)} %add.246, f32[]{:T(128)} %constant.88.clone.1), padding=0_0_0x1_0_1x0_0_0x0_0_0 | pad | bytes 3145732 | tf_op jit(solution)/shard_map/pad | solution.py:57
  76.7 2.2 pad.92
  78.9 3.0 %pad.93 = f32[1,8,256,256]{3,2,1,0:T(8,128)} pad(f32[1,4,256,256]{3,2,1,0:T(8,128)S(1)} %copy-done.8, f32[]{:T(128)} %constant.88.clone.1), padding=0_0_0x1_0_1x0_0_0x0_0_0 | pad | bytes 3145732 | tf_op jit(solution)/shard_map/pad | solution.py:60
  81.9 3.3 %add.260 = f32[1,8,256,256]{3,2,1,0:T(8,128)} add(f32[1,8,256,256]{3,2,1,0:T(8,128)S(1)} %pad.92, f32[1,8,256,256]{3,2,1,0:T(8,128)} %pad.93) | non-fusion elementwise | flops 524288 | bytes 6291456 | tf_op jit(solution)/shard_map/add | solution.py:60
  85.2 3.1 %rev.12 = f32[1,8,256,256]{3,2,1,0:T(8,128)} reverse(f32[1,8,256,256]{3,2,1,0:T(8,128)} %add.260), dimensions={1} | reverse | bytes 4194304 | tf_op jit(solution)/shard_map/jit(_flip)/rev | solution.py:63
  88.3 7.4 %all_gather.13 = f32[4,1,256]{2,1,0:T(1,128)S(1)} all-gather(f32[1,1,256]{2,1,0:T(1,128)S(1)} %slice_add_fusion.3), channel_id=1, replica_groups=mesh['grp'=2,'step'=4,'chain'=2,'rep'=2] {'step'}, dimensions={0}, use_global_device_ids=true | all-gather | bytes 5120 | tf_op jit(solution)/shard_map/all_gather | solution.py:15
  95.6 6.8 %all_gather.15 = f32[4,1,256]{2,1,0:T(1,128)S(1)} all-gather(f32[1,1,256]{2,1,0:T(1,128)S(1)} %slice_add_fusion.2), channel_id=1, replica_groups=mesh['grp'=2,'step'=4,'chain'=2,'rep'=2] {'step'}, dimensions={0}, use_global_device_ids=true | all-gather | bytes 5120 | tf_op jit(solution)/shard_map/all_gather | solution.py:15
  104.2 11.0 %while.33 = (s32[]{:T(128)}, f32[1,256,256]{2,1,0:T(8,128)S(1)}, f32[1,256]{1,0:T(1,128)S(1)}, s32[]{:T(128)}, f32[4,1,256,256]{3,2,1,0:T(8,128)}, /*index=5*/f32[4,1,256]{2,1,0:T(1,128)S(1)}, s32[]{:T(128)}, s32[]{:T(128)}) while((s32[]{:T(128)}, f32[1,256,256]{2,1,0:T(8,128)S(1)}, f32[1,256]{1,0:T(1,128)S(1)}, s32[]{:T(128)}, ...), condition=%wide.region_1.2_spmd.clone, body=%wide.region_0.1_spmd.clone.sunk | while | flops 202179584 | bytes 1845375 | solution.py:26
  116.2 3.5 %fusion.19 = f32[1,8,256]{2,0,1:T(1,128)S(1)} fusion(f32[256,1,1]{0,1,2:T(1,128)S(1)} %fusion.28, f32[1,8,256,256]{3,2,1,0:T(8,128)S(1)} %copy-done.2, f32[1,8,256,256]{3,2,1,0:T(8,128)} %pad.81), kind=kOutput, calls=%fused_computation.27 | convolution fusion | flops 6815744 | bytes 4203520 | tf_op jit(solution)/shard_map/ctij,cj->cti/dot_general | solution.py:74
  119.8 14.8 %all-gather.5.cloned.1.call-done = f32[4,1,256,256]{3,2,1,0:T(8,128)} async-done(((f32[1,1,256,256]{3,2,1,0:T(8,128)}), f32[4,1,256,256]{3,2,1,0:T(8,128)}) %all-gather.5.cloned.1.call-update) | async-done | bytes 1048592 | tf_op jit(solution)/shard_map/all_gather | solution.py:15
  134.6 5.3 %while.34 = (s32[]{:T(128)}, f32[1,256]{1,0:T(1,128)S(1)}, s32[]{:T(128)}, f32[4,1,256,256]{3,2,1,0:T(8,128)}, f32[4,1,256]{2,1,0:T(1,128)S(1)}, /*index=5*/s32[]{:T(128)}, s32[]{:T(128)}, s32[]{:T(128)}, s32[]{:T(128)}) while((s32[]{:T(128)}, f32[1,256]{1,0:T(1,128)S(1)}, s32[]{:T(128)}, f32[4,1,256,256]{3,2,1,0:T(8,128)}, ...), condition=%wide.region_3.4_spmd.clone, body=%wide.region_2.3_spmd.clone.sunk | while | flops 787464 | bytes 272560 | solution.py:26
  139.9 3.4 %fusion.17 = f32[1,8,256]{2,0,1:T(1,128)S(1)} fusion(f32[1,8,256,256]{3,2,1,0:T(8,128)} %rev.12, f32[1,256]{1,0:T(1,128)S(1)} %get-tuple-element.247), kind=kOutput, calls=%fused_computation.25 | convolution fusion | flops 6291456 | bytes 2106368 | tf_op jit(solution)/shard_map/ctij,cj->cti/dot_general | solution.py:75
  143.4 30.3 %psum.15 = f32[256]{0:T(256)} all-reduce(f32[256]{0:T(256)S(1)} %broadcast_multiply_fusion), channel_id=1, replica_groups=mesh['grp'=2,'step'=4,'chain'=2,'rep'=2] {'step','chain','rep'}, use_global_device_ids=true, to_apply=%region_6.7 | all-reduce | flops 256 | bytes 2048 | tf_op jit(solution)/shard_map/psum | solution.py:81
  175.5 88.6 %all-reduce.26.cloned.1.call-done = f32[256,256]{1,0:T(8,128)} async-done(((f32[256,256]{1,0:T(8,128)}), f32[256,256]{1,0:T(8,128)}) %all-reduce.26.cloned.1.call-update) | async-done | bytes 262160 | tf_op jit(solution)/shard_map/psum | solution.py:81
  (187 shorter events, 58.0 us)
Async XLA Ops:
  7.2 14.3 %copy-start.9 = (f32[256,256]{1,0:T(8,128)S(1)}, f32[256,256]{1,0:T(8,128)}, u32[]{:S(2)}) copy-start(f32[256,256]{1,0:T(8,128)} %param.17) | copy-start | bytes 786436
  7.2 97.0 %all-gather.3.cloned.1.call-start = ((), (), s32[]{:S(2)}) async-start(), calls=%async_computation | async-start | bytes 1310720 | tf_op jit(solution)/shard_map/all_gather | solution.py:15
  8.0 8.2 %collective-permute-start = (f32[1,256]{1,0:T(1,128)S(1)}, f32[1,256]{1,0:T(1,128)S(1)}, u32[]{:S(2)}, u32[]{:S(2)}) collective-permute-start(f32[1,256]{1,0:T(1,128)S(1)} %slice_bitcast_fusion.12), channel_id=1, source_target_pairs={{0,4},{4,8},{8,12},{1,5},{5,9},{9,13},{2,6},{6,10},{10,14},{3,7},{... | collective-permute-start | bytes 3080 | tf_op jit(solution)/shard_map/ppermute | solution.py:10
  24.2 9.1 %copy-start.12 = (f32[1,4,256]{2,1,0:T(4,128)}, f32[1,4,256]{2,1,0:T(4,128)S(1)}, u32[]{:S(2)}) copy-start(f32[1,4,256]{2,1,0:T(4,128)S(1)} %bitcast_add_fusion.3) | copy-start | bytes 12292
  24.2 2.8 %copy-start = (f32[1,8,256,256]{2,3,1,0:T(8,128)S(1)}, f32[1,8,256,256]{2,3,1,0:T(8,128)}, u32[]{:S(2)}) copy-start(f32[1,8,256,256]{2,3,1,0:T(8,128)} %get-tuple-element.324) | copy-start | bytes 6291460
  29.8 1.9 copy-start.3
  30.5 21.2 %copy-start.11 = (f32[1,4,256]{2,1,0:T(4,128)}, f32[1,4,256]{2,1,0:T(4,128)S(1)}, u32[]{:S(2)}) copy-start(f32[1,4,256]{2,1,0:T(4,128)S(1)} %bitcast_add_fusion.1) | copy-start | bytes 12292
  40.1 3.1 %copy-start.4 = (f32[1,4,256,256]{3,2,1,0:T(8,128)S(1)}, f32[1,4,256,256]{3,2,1,0:T(8,128)}, u32[]{:S(2)}) copy-start(f32[1,4,256,256]{3,2,1,0:T(8,128)} %pad.79) | copy-start | bytes 3145732
  50.0 4.3 %slice-start.1 = ((f32[1,4,256]{2,1,0:T(4,128)}), f32[1,1,256]{2,1,0:T(1,128)S(1)}, s32[]{:S(2)}) async-start(f32[1,4,256]{2,1,0:T(4,128)} %copy-done.12), calls=%async_computation.4 | async-start | bytes 2048 | tf_op jit(solution)/shard_map/slice | solution.py:57
  50.7 0.8 copy-start.6
  59.5 6.5 %copy-start.1 = (f32[1,8,256,256]{3,2,1,0:T(8,128)}, f32[1,8,256,256]{3,2,1,0:T(8,128)S(1)}, u32[]{:S(2)}) copy-start(f32[1,8,256,256]{3,2,1,0:T(8,128)S(1)} %pad.80) | copy-start | bytes 6291460
  59.6 6.5 %slice-start = ((f32[1,4,256]{2,1,0:T(4,128)}), f32[1,1,256]{2,1,0:T(1,128)S(1)}, s32[]{:S(2)}) async-start(f32[1,4,256]{2,1,0:T(4,128)} %copy-done.11), calls=%async_computation.3 | async-start | bytes 2048 | tf_op jit(solution)/shard_map/slice | solution.py:60
  66.0 68.6 %all-gather.5.cloned.1.call-start = ((), (), s32[]{:S(2)}) async-start(), calls=%async_computation.1 | async-start | bytes 1310720 | tf_op jit(solution)/shard_map/all_gather | solution.py:15
  66.1 2.8 %copy-start.7 = (f32[1,2,256,256]{3,2,1,0:T(8,128)S(1)}, f32[1,2,256,256]{3,2,1,0:T(8,128)}, u32[]{:S(2)}) copy-start(f32[1,2,256,256]{3,2,1,0:T(8,128)} %copy-done.6) | copy-start | bytes 1572868
  71.9 2.3 copy-start.5
  74.2 1.4 copy-start.10
  76.7 2.3 copy-start.8
  104.1 12.1 %copy-start.2 = (f32[1,8,256,256]{3,2,1,0:T(8,128)S(1)}, f32[1,8,256,256]{3,2,1,0:T(8,128)}, u32[]{:S(2)}) copy-start(f32[1,8,256,256]{3,2,1,0:T(8,128)} %copy-done.1) | copy-start | bytes 6291460
  104.2 159.9 %all-reduce.26.cloned.1.call-start = ((), (), s32[]{:S(2)}) async-start(), calls=%async_computation.2 | async-start | bytes 524288 | tf_op jit(solution)/shard_map/psum | solution.py:81
  119.7 23.6 %copy-start.14 = (f32[1,8,256]{2,1,0:T(8,128)S(1)}, f32[1,8,256]{2,1,0:T(8,128)}, u32[]{:S(2)}) copy-start(f32[1,8,256]{2,1,0:T(8,128)} %param.21) | copy-start | bytes 24580
  119.7 23.6 %copy-start.15 = (f32[256]{0:T(256)S(1)}, f32[256]{0:T(256)}, u32[]{:S(2)}) copy-start(f32[256]{0:T(256)} %param.18) | copy-start | bytes 3076
  119.7 54.0 %copy-start.13 = (f32[1,8,256]{2,1,0:T(8,128)S(1)}, f32[1,8,256]{2,1,0:T(8,128)}, u32[]{:S(2)}) copy-start(f32[1,8,256]{2,1,0:T(8,128)} %param.20) | copy-start | bytes 24580
Sparse Core Ops, SparseCore 0:
  66.1 28.3 all-gather.2
  104.3 30.2 all-gather.4
  175.0 89.0 all-reduce.25
where the time goes:
time: 274 us; the launch traced here: 272 us
  waiting for transfers between devices  104 us (38%)
  matrix products  46 us (17%)
  blocking collectives  44.4 us (16%)
  local copies, waits for them, and re-layouts  38.7 us (14%)
  other arithmetic  19.8 us (7%)
  between operations  15.1 us (6%)
  starting transfers between devices  4.14 us (2%)
    psum x1, waiting for transfers between devices, shards(): lax.psum((grad_local, bias_local), ('step', 'chain', 'rep'))  88.6 us
    psum x1, blocking collectives, shards(): lax.psum((grad_local, bias_local), ('step', 'chain', 'rep'))  30.3 us
    dot_general x14, matrix products, compose(): jnp.einsum('...ij,...jk->...ik', late_mat, early_mat, precision=highest)  17.2 us
    dot_general x18, matrix products, compose(): jnp.einsum('...ij,...j->...i', late_mat, early_vec, precision=highest)  16.1 us
    all_gather x2, waiting for transfers between devices, carried_in(): everything = jax.tree.map(lambda part: lax.all_gather(part, axis), x)  14.8 us
    all_gather x2, blocking collectives, carried_in(): everything = jax.tree.map(lambda part: lax.all_gather(part, axis), x)  14.2 us
    slice x18, local copies, waits for them, and re-layouts, shards(): lax.associative_scan(compose, (jnp.flip(transposed, 1), jnp.flip(source,...  11.3 us
    pad x8, local copies, waits for them, and re-layouts, shards(): lax.associative_scan(compose, (jacobian, offset), axis=1)  10.9 us
  transfers between devices with their start and end apart: 4, of which 2 were waited for; matrix products, arithmetic and copies ran while one was open for 16% of the time, Pallas kernels for 0%

commit v1 on v0

--- a/solution.py
+++ b/solution.py
@@ -78,7 +78,7 @@
     weighted = adjoint * slope
     grad_local = step_size * jnp.einsum("cti,ctj->ij", weighted, previous, precision=highest)
     bias_local = step_size * jnp.sum(weighted, axis=(0, 1))
-    grad_w, grad_b = lax.psum((grad_local, bias_local), ("step", "chain", "rep"))
+    grad_w, grad_b = lax.psum(lax.psum((grad_local, bias_local), ("chain", "rep")), "step")
     return (path_new, grad_w, grad_b)
 
 

time: 274 us -> 225 us (0.82)
  waiting for transfers between devices: 104 us -> 65.1 us
  blocking collectives: 44.4 us -> 31.5 us
    psum x1 -> x2, waiting for transfers between devices: 88.6 us -> 45.4 us  [the longest x1 25.7 us: shards(): lax.psum((grad_local, bias_local), ('chain', 'rep'))]
    psum x1 -> x2, blocking collectives: 30.3 us -> 17.4 us  [the longest x1 10.2 us: shards(): lax.psum(lax.psum((grad_local, bias_local), ('chain', 'rep')), 'step')]
    all_gather x2, waiting for transfers between devices: 14.8 us -> 19.6 us  [carried_in(): everything = jax.tree.map(lambda part: lax.all_gather(part, axis), x)]
  transfers between devices with their start and end apart: 4 -> 5, of which waited for: 2 -> 3; matrix products, arithmetic and copies ran while one was open for 16% -> 19% of each run, Pallas kernels for 0% -> 0%
where the time goes in v1:
time: 225 us; the launch traced here: 221 us
  waiting for transfers between devices  65.1 us (29%)
  matrix products  46 us (20%)
  local copies, waits for them, and re-layouts  38.7 us (17%)
  blocking collectives  31.5 us (14%)
  other arithmetic  19.8 us (9%)
  between operations  15.1 us (7%)
  starting transfers between devices  4.18 us (2%)
    psum x1, waiting for transfers between devices, shards(): lax.psum((grad_local, bias_local), ('chain', 'rep'))  25.7 us
    psum x1, waiting for transfers between devices, shards(): lax.psum(lax.psum((grad_local, bias_local), ('chain', 'rep')), 'step')  19.8 us
    all_gather x2, waiting for transfers between devices, carried_in(): everything = jax.tree.map(lambda part: lax.all_gather(part, axis), x)  19.6 us
    dot_general x14, matrix products, compose(): jnp.einsum('...ij,...jk->...ik', late_mat, early_mat, precision=highest)  17.2 us
    dot_general x18, matrix products, compose(): jnp.einsum('...ij,...j->...i', late_mat, early_vec, precision=highest)  16.2 us
    all_gather x2, blocking collectives, carried_in(): everything = jax.tree.map(lambda part: lax.all_gather(part, axis), x)  14.1 us
    slice x18, local copies, waits for them, and re-layouts, shards(): lax.associative_scan(compose, (jnp.flip(transposed, 1), jnp.flip(source,...  11.3 us
    pad x8, local copies, waits for them, and re-layouts, shards(): lax.associative_scan(compose, (jacobian, offset), axis=1)  10.9 us
  transfers between devices with their start and end apart: 5, of which 3 were waited for; matrix products, arithmetic and copies ran while one was open for 19% of the time, Pallas kernels for 0%

profile of v1, /device:TPU:1, one launch (start us, length us, event | category | flops | bytes accessed | tf_op | source)
XLA Modules:
  0.0 221.0 jit_solution(8549606624488524329)
XLA Ops:
  8.0 4.0 %collective-permute-start = (f32[1,256]{1,0:T(1,128)S(1)}, f32[1,256]{1,0:T(1,128)S(1)}, u32[]{:S(2)}, u32[]{:S(2)}) collective-permute-start(f32[1,256]{1,0:T(1,128)S(1)} %slice_bitcast_fusion.12), channel_id=1, source_target_pairs={{0,4},{4,8},{8,12},{1,5},{5,9},{9,13},{2,6},{6,10},{10,14},{3,7},{... | collective-permute-start | bytes 3080 | tf_op jit(solution)/shard_map/ppermute | solution.py:10
  13.4 2.8 %gather_fusion = f32[8,256]{1,0:T(8,128)S(1)} fusion(f32[4096,256]{1,0:T(8,128)} %param.16, s32[1024]{0:T(1024)S(1)} %pad_clamp_fusion), kind=kCustom, calls=%fused_computation | custom fusion | bytes 16416 | tf_op jit(solution)/shard_map/gather | solution.py:51
  18.9 2.4 %fusion.21 = f32[8,1,256]{2,1,0:T(1,128)S(1)} fusion(f32[256,256]{1,0:T(8,128)} %param.17, f32[8,256]{1,0:T(8,128)S(1)} %get-tuple-element.327, f32[256,256]{1,0:T(8,128)S(1)} %fusion.81, f32[8,256]{1,0:T(8,128)S(1)} %get-tuple-element.328, f32[8,256,1]{1,0,2:T(8,128)} %bitcast.301), kind=kOutput, calls=%fused_computation.29 | convolution fusion | flops 7864320 | bytes 557056 | tf_op jit(solution)/shard_map/ctij,ctj->cti/dot_general | solution.py:59
  37.3 2.8 %pad.79 = f32[1,4,256,256]{3,2,1,0:T(8,128)} pad(f32[1,2,256,256]{3,2,1,0:T(8,128)} %pad_add_fusion.1, f32[]{:T(128)} %constant.88.clone.1), padding=0_0_0x1_0_1x0_0_0x0_0_0 | pad | bytes 1572868 | tf_op jit(solution)/shard_map/pad | solution.py:57
  40.0 3.1 %convolution_bitcast_fusion.4 = f32[1,3,256,256]{3,2,1,0:T(8,128)} fusion(f32[1,4,256,256]{3,2,1,0:T(8,128)} %pad.79, f32[1,4,256,256]{3,2,1,0:T(8,128)S(1)} %pad.78, f32[1,8,256,256]{3,2,1,0:T(8,128)S(1)} %get-tuple-element.325), kind=kOutput, calls=%fused_computation.38 | convolution fusion | flops 604176384 | bytes 3145728 | tf_op jit(solution)/shard_map/...ij,...jk->...ik/dot_general | solution.py:33
  44.2 2.3 %slice.227 = f32[1,4,256,256]{2,3,1,0:T(8,128)} reverse(f32[1,4,256,256]{2,3,1,0:T(8,128)} %get-tuple-element.323), dimensions={1} | reverse | bytes 2097152 | tf_op jit(solution)/shard_map/slice | solution.py:60
  46.5 3.4 %convolution_bitcast_fusion.1 = f32[1,4,256,256]{3,2,1,0:T(8,128)S(1)} fusion(f32[1,4,256,256]{2,3,1,0:T(8,128)} %slice.227, f32[1,4,256,256]{2,3,1,0:T(8,128)} %copy-done.3), kind=kOutput, calls=%fused_computation.35 | convolution fusion | flops 805306368 | bytes 3145728 | tf_op jit(solution)/shard_map/...ij,...jk->...ik/dot_general | solution.py:33
  55.0 2.3 %pad_maximum_fusion = f32[1,4,256,256]{3,2,1,0:T(8,128)} fusion(f32[1,3,256,256]{3,2,1,0:T(8,128)} %convolution_bitcast_fusion.4, f32[1,1,256,256]{3,2,1,0:T(8,128)} %slice.260), kind=kLoop, calls=%fused_computation.56 | loop fusion | flops 262144 | bytes 2097152 | tf_op jit(solution)/shard_map/concatenate | solution.py:57
  59.5 4.7 %pad.81 = f32[1,8,256,256]{3,2,1,0:T(8,128)} pad(f32[1,4,256,256]{3,2,1,0:T(8,128)} %add.250, f32[]{:T(128)} %constant.88.clone.1), padding=0_0_0x1_0_1x0_0_0x0_0_0 | pad | bytes 3145732 | tf_op jit(solution)/shard_map/pad | solution.py:57
  76.7 2.2 %pad.92 = f32[1,8,256,256]{3,2,1,0:T(8,128)S(1)} pad(f32[1,4,256,256]{3,2,1,0:T(8,128)} %pad_maximum_fusion.1, f32[]{:T(128)} %constant.88.clone.1), padding=0_0_0x0_1_1x0_0_0x0_0_0 | pad | bytes 3145732 | tf_op jit(solution)/shard_map/pad | solution.py:60
  79.0 3.0 %pad.93 = f32[1,8,256,256]{3,2,1,0:T(8,128)} pad(f32[1,4,256,256]{3,2,1,0:T(8,128)S(1)} %copy-done.8, f32[]{:T(128)} %constant.88.clone.1), padding=0_0_0x1_0_1x0_0_0x0_0_0 | pad | bytes 3145732 | tf_op jit(solution)/shard_map/pad | solution.py:60
  81.9 3.3 %add.264 = f32[1,8,256,256]{3,2,1,0:T(8,128)} add(f32[1,8,256,256]{3,2,1,0:T(8,128)S(1)} %pad.92, f32[1,8,256,256]{3,2,1,0:T(8,128)} %pad.93) | non-fusion elementwise | flops 524288 | bytes 6291456 | tf_op jit(solution)/shard_map/add | solution.py:60
  85.2 3.1 %rev.12 = f32[1,8,256,256]{3,2,1,0:T(8,128)} reverse(f32[1,8,256,256]{3,2,1,0:T(8,128)} %add.264), dimensions={1} | reverse | bytes 4194304 | tf_op jit(solution)/shard_map/jit(_flip)/rev | solution.py:63
  88.3 7.3 %all_gather.13 = f32[4,1,256]{2,1,0:T(1,128)S(1)} all-gather(f32[1,1,256]{2,1,0:T(1,128)S(1)} %slice_add_fusion.3), channel_id=1, replica_groups=mesh['grp'=2,'step'=4,'chain'=2,'rep'=2] {'step'}, dimensions={0}, use_global_device_ids=true | all-gather | bytes 5120 | tf_op jit(solution)/shard_map/all_gather | solution.py:15
  95.6 6.7 %all_gather.15 = f32[4,1,256]{2,1,0:T(1,128)S(1)} all-gather(f32[1,1,256]{2,1,0:T(1,128)S(1)} %slice_add_fusion.2), channel_id=1, replica_groups=mesh['grp'=2,'step'=4,'chain'=2,'rep'=2] {'step'}, dimensions={0}, use_global_device_ids=true | all-gather | bytes 5120 | tf_op jit(solution)/shard_map/all_gather | solution.py:15
  104.2 10.8 %while.33 = (s32[]{:T(128)}, f32[1,256,256]{2,1,0:T(8,128)S(1)}, f32[1,256]{1,0:T(1,128)S(1)}, s32[]{:T(128)}, f32[4,1,256,256]{3,2,1,0:T(8,128)}, /*index=5*/f32[4,1,256]{2,1,0:T(1,128)S(1)}, s32[]{:T(128)}, s32[]{:T(128)}) while((s32[]{:T(128)}, f32[1,256,256]{2,1,0:T(8,128)S(1)}, f32[1,256]{1,0:T(1,128)S(1)}, s32[]{:T(128)}, ...), condition=%wide.region_1.2_spmd.clone, body=%wide.region_0.1_spmd.clone.sunk | while | flops 202179584 | bytes 1845375 | solution.py:26
  115.0 19.6 %all-gather.5.cloned.1.call-done = f32[4,1,256,256]{3,2,1,0:T(8,128)} async-done(((f32[1,1,256,256]{3,2,1,0:T(8,128)}), f32[4,1,256,256]{3,2,1,0:T(8,128)}) %all-gather.5.cloned.1.call-update) | async-done | bytes 1048592 | tf_op jit(solution)/shard_map/all_gather | solution.py:15
  134.6 5.5 %while.34 = (s32[]{:T(128)}, f32[1,256]{1,0:T(1,128)S(1)}, s32[]{:T(128)}, f32[4,1,256,256]{3,2,1,0:T(8,128)}, f32[4,1,256]{2,1,0:T(1,128)S(1)}, /*index=5*/s32[]{:T(128)}, s32[]{:T(128)}, s32[]{:T(128)}, s32[]{:T(128)}) while((s32[]{:T(128)}, f32[1,256]{1,0:T(1,128)S(1)}, s32[]{:T(128)}, f32[4,1,256,256]{3,2,1,0:T(8,128)}, ...), condition=%wide.region_3.4_spmd.clone, body=%wide.region_2.3_spmd.clone.sunk | while | flops 787464 | bytes 272560 | solution.py:26
  140.1 3.4 %fusion.17 = f32[1,8,256]{2,0,1:T(1,128)S(1)} fusion(f32[1,8,256,256]{3,2,1,0:T(8,128)} %rev.12, f32[1,256]{1,0:T(1,128)S(1)} %get-tuple-element.247), kind=kOutput, calls=%fused_computation.25 | convolution fusion | flops 6291456 | bytes 2106368 | tf_op jit(solution)/shard_map/ctij,cj->cti/dot_general | solution.py:75
  145.9 3.5 %fusion.19 = f32[1,8,256]{2,0,1:T(1,128)S(1)} fusion(f32[256,1,1]{0,1,2:T(1,128)S(1)} %fusion.28, f32[1,8,256,256]{3,2,1,0:T(8,128)S(1)} %copy-done.2, f32[1,8,256,256]{3,2,1,0:T(8,128)} %pad.81), kind=kOutput, calls=%fused_computation.27 | convolution fusion | flops 6815744 | bytes 4203520 | tf_op jit(solution)/shard_map/ctij,cj->cti/dot_general | solution.py:74
  149.4 25.7 %all-reduce.27.cloned.1.call-done = f32[256,256]{1,0:T(8,128)} async-done(((f32[256,256]{1,0:T(8,128)}), f32[256,256]{1,0:T(8,128)}) %all-reduce.27.cloned.1.call-update) | async-done | bytes 262160 | tf_op jit(solution)/shard_map/psum | solution.py:81
  175.1 7.2 %psum.30 = f32[256]{0:T(256)S(1)} all-reduce(f32[256]{0:T(256)S(1)} %broadcast_multiply_fusion), channel_id=1, replica_groups=mesh['grp'=2,'step'=4,'chain'=2,'rep'=2] {'chain','rep'}, use_global_device_ids=true, to_apply=%region_7.8 | all-reduce | flops 256 | bytes 2048 | tf_op jit(solution)/shard_map/psum | solution.py:81
  182.3 10.2 %psum.31 = f32[256]{0:T(256)} all-reduce(f32[256]{0:T(256)S(1)} %psum.30), channel_id=1, replica_groups=mesh['grp'=2,'step'=4,'chain'=2,'rep'=2] {'step'}, use_global_device_ids=true, to_apply=%region_8.9 | all-reduce | flops 256 | bytes 2048 | tf_op jit(solution)/shard_map/psum | solution.py:81
  193.1 19.8 %all-reduce.29.cloned.1.call-done = f32[256,256]{1,0:T(8,128)} async-done(((f32[256,256]{1,0:T(8,128)}), f32[256,256]{1,0:T(8,128)}) %all-reduce.29.cloned.1.call-update) | async-done | bytes 262160 | tf_op jit(solution)/shard_map/psum | solution.py:81
  (191 shorter events, 62.4 us)
Async XLA Ops:
  7.2 14.3 %copy-start.9 = (f32[256,256]{1,0:T(8,128)S(1)}, f32[256,256]{1,0:T(8,128)}, u32[]{:S(2)}) copy-start(f32[256,256]{1,0:T(8,128)} %param.17) | copy-start | bytes 786436
  7.2 97.0 %all-gather.3.cloned.1.call-start = ((), (), s32[]{:S(2)}) async-start(), calls=%async_computation | async-start | bytes 1310720 | tf_op jit(solution)/shard_map/all_gather | solution.py:15
  8.0 8.2 %collective-permute-start = (f32[1,256]{1,0:T(1,128)S(1)}, f32[1,256]{1,0:T(1,128)S(1)}, u32[]{:S(2)}, u32[]{:S(2)}) collective-permute-start(f32[1,256]{1,0:T(1,128)S(1)} %slice_bitcast_fusion.12), channel_id=1, source_target_pairs={{0,4},{4,8},{8,12},{1,5},{5,9},{9,13},{2,6},{6,10},{10,14},{3,7},{... | collective-permute-start | bytes 3080 | tf_op jit(solution)/shard_map/ppermute | solution.py:10
  24.2 9.1 %copy-start.12 = (f32[1,4,256]{2,1,0:T(4,128)}, f32[1,4,256]{2,1,0:T(4,128)S(1)}, u32[]{:S(2)}) copy-start(f32[1,4,256]{2,1,0:T(4,128)S(1)} %bitcast_add_fusion.3) | copy-start | bytes 12292
  24.2 2.8 %copy-start = (f32[1,8,256,256]{2,3,1,0:T(8,128)S(1)}, f32[1,8,256,256]{2,3,1,0:T(8,128)}, u32[]{:S(2)}) copy-start(f32[1,8,256,256]{2,3,1,0:T(8,128)} %get-tuple-element.324) | copy-start | bytes 6291460
  29.8 1.9 copy-start.3
  30.5 21.2 %copy-start.11 = (f32[1,4,256]{2,1,0:T(4,128)}, f32[1,4,256]{2,1,0:T(4,128)S(1)}, u32[]{:S(2)}) copy-start(f32[1,4,256]{2,1,0:T(4,128)S(1)} %bitcast_add_fusion.1) | copy-start | bytes 12292
  40.0 3.1 %copy-start.4 = (f32[1,4,256,256]{3,2,1,0:T(8,128)S(1)}, f32[1,4,256,256]{3,2,1,0:T(8,128)}, u32[]{:S(2)}) copy-start(f32[1,4,256,256]{3,2,1,0:T(8,128)} %pad.79) | copy-start | bytes 3145732
  49.9 4.3 %slice-start.1 = ((f32[1,4,256]{2,1,0:T(4,128)}), f32[1,1,256]{2,1,0:T(1,128)S(1)}, s32[]{:S(2)}) async-start(f32[1,4,256]{2,1,0:T(4,128)} %copy-done.12), calls=%async_computation.5 | async-start | bytes 2048 | tf_op jit(solution)/shard_map/slice | solution.py:57
  50.6 0.8 copy-start.6
  59.5 6.5 %copy-start.1 = (f32[1,8,256,256]{3,2,1,0:T(8,128)}, f32[1,8,256,256]{3,2,1,0:T(8,128)S(1)}, u32[]{:S(2)}) copy-start(f32[1,8,256,256]{3,2,1,0:T(8,128)S(1)} %pad.80) | copy-start | bytes 6291460
  59.5 6.5 %slice-start = ((f32[1,4,256]{2,1,0:T(4,128)}), f32[1,1,256]{2,1,0:T(1,128)S(1)}, s32[]{:S(2)}) async-start(f32[1,4,256]{2,1,0:T(4,128)} %copy-done.11), calls=%async_computation.4 | async-start | bytes 2048 | tf_op jit(solution)/shard_map/slice | solution.py:60
  66.0 68.6 %all-gather.5.cloned.1.call-start = ((), (), s32[]{:S(2)}) async-start(), calls=%async_computation.1 | async-start | bytes 1310720 | tf_op jit(solution)/shard_map/all_gather | solution.py:15
  66.0 2.8 %copy-start.7 = (f32[1,2,256,256]{3,2,1,0:T(8,128)S(1)}, f32[1,2,256,256]{3,2,1,0:T(8,128)}, u32[]{:S(2)}) copy-start(f32[1,2,256,256]{3,2,1,0:T(8,128)} %copy-done.6) | copy-start | bytes 1572868
  71.9 2.3 %copy-start.5 = (f32[1,3,256,256]{2,3,1,0:T(8,128)S(1)}, f32[1,3,256,256]{2,3,1,0:T(8,128)}, u32[]{:S(2)}) copy-start(f32[1,3,256,256]{2,3,1,0:T(8,128)} %slice.223) | copy-start | bytes 2359300
  74.2 1.4 copy-start.10
  76.7 2.3 %copy-start.8 = (f32[1,4,256,256]{3,2,1,0:T(8,128)S(1)}, f32[1,4,256,256]{3,2,1,0:T(8,128)}, u32[]{:S(2)}) copy-start(f32[1,4,256,256]{3,2,1,0:T(8,128)} %add.263) | copy-start | bytes 3145732
  104.1 70.9 %all-reduce.27.cloned.1.call-start = ((), (), s32[]{:S(2)}) async-start(), calls=%async_computation.2 | async-start | bytes 524288 | tf_op jit(solution)/shard_map/psum | solution.py:81
  115.0 28.6 %copy-start.14 = (f32[1,8,256]{2,1,0:T(8,128)S(1)}, f32[1,8,256]{2,1,0:T(8,128)}, u32[]{:S(2)}) copy-start(f32[1,8,256]{2,1,0:T(8,128)} %param.21) | copy-start | bytes 24580
  115.0 28.5 %copy-start.15 = (f32[256]{0:T(256)S(1)}, f32[256]{0:T(256)}, u32[]{:S(2)}) copy-start(f32[256]{0:T(256)} %param.18) | copy-start | bytes 3076
  115.0 28.6 %copy-start.13 = (f32[1,8,256]{2,1,0:T(8,128)S(1)}, f32[1,8,256]{2,1,0:T(8,128)}, u32[]{:S(2)}) copy-start(f32[1,8,256]{2,1,0:T(8,128)} %param.20) | copy-start | bytes 24580
  134.6 11.2 %copy-start.2 = (f32[1,8,256,256]{3,2,1,0:T(8,128)S(1)}, f32[1,8,256,256]{3,2,1,0:T(8,128)}, u32[]{:S(2)}) copy-start(f32[1,8,256,256]{3,2,1,0:T(8,128)} %copy-done.1) | copy-start | bytes 6291460
  144.8 68.1 %all-reduce.29.cloned.1.call-start = ((), (), s32[]{:S(2)}) async-start(), calls=%async_computation.3 | async-start | bytes 524288 | tf_op jit(solution)/shard_map/psum | solution.py:81
Sparse Core Ops, SparseCore 0:
  66.1 28.3 all-gather.2
  104.2 30.3 all-gather.4
  144.9 30.0 all-reduce.26
  177.3 35.4 all-reduce.28
